TPU v7x, 32 devices: a whole 2x2x4 slice. The times are simulated.
32 devices in a mesh: ctx: 16 (over z, y, x), tp: 2 (over core).
Axes of the slice: x: 2, y: 2, z: 4, core: 2. Of those that a mesh axis runs over, the one named last changes fastest.
Arguments:
- tokens: bfloat16 [4096, 4096], P('ctx', 'tp'), may hold values from -6 to 6
- norm_gain: bfloat16 [4096], P('tp'), may hold values from 0.25 to 1.75
- doc_ids: int32 [4096], P('ctx'), may hold values from 0 to 3, never falling along the last dimension, each value on 1 to 3840 neighbouring positions
- q_weight: bfloat16 [4096, 4096], P('ctx', 'tp'), may hold values from -0.09375 to 0.09375
- k_weight: bfloat16 [4096, 1024], P('ctx', 'tp'), may hold values from -0.09375 to 0.09375
- v_weight: bfloat16 [4096, 1024], P('ctx', 'tp'), may hold values from -0.09375 to 0.09375
- o_weight: bfloat16 [4096, 4096], P('tp', 'ctx'), may hold values from -0.09375 to 0.09375
Outputs:
- mixed: bfloat16 [4096, 4096], P('ctx', 'tp')
Inputs may be any that keep to these rules, and one draw needn't show every extreme that they name: `doc_ids`: non-decreasing along the sequence; each document is a run of at most 3840 tokens and one run has exactly 3840.
All inputs are finite; a program needn't handle non-finite values.
Results may differ from a plain program's by a relative error of at most 0.015.
Values may be sent and summed in bfloat16 or wider, within the bound.
A program may use at most 128 MiB of HBM per device.

v0:
```python
import jax
import jax.numpy as jnp
from jax import lax
from jax.sharding import PartitionSpec as P

HEAD = 128
WIN = 16


def shifted(block, axis, distance):
    devices = range(lax.axis_size(axis))
    route = [(i - distance, i) for i in devices if i - distance in devices]
    return lax.ppermute(block, axis, route)


def rotate(values, positions):
    half_dim = values.shape[-1] // 2
    inv_freq = 500000.0 ** (-(jnp.arange(half_dim, dtype=jnp.float32) * 2.0) / values.shape[-1])
    angles = positions[:, None] * inv_freq[None, :]
    cos_part = jnp.cos(angles)[:, None, :]
    sin_part = jnp.sin(angles)[:, None, :]
    first_half = values[..., :half_dim]
    second_half = values[..., half_dim:]
    return jnp.concatenate(
        [
            first_half * cos_part - second_half * sin_part,
            second_half * cos_part + first_half * sin_part,
        ],
        axis=-1,
    )


def local(tokens, norm_gain, doc_ids, q_weight, k_weight, v_weight, o_weight):
    tok_rows = tokens.shape[0]
    whole, gain_whole = (
        lax.all_gather(tokens, "tp", axis=1, tiled=True),
        lax.all_gather(norm_gain, "tp", axis=0, tiled=True),
    )
    x_float = whole.astype(jnp.float32)
    mean_sq = jnp.mean(x_float * x_float, axis=-1, keepdims=True)
    normed = (x_float * lax.rsqrt(mean_sq + 1e-05) * gain_whole.astype(jnp.float32)).astype(
        jnp.bfloat16
    )
    q_cols = q_weight.shape[1]
    kv_cols = k_weight.shape[1]
    pieces = (
        lax.all_gather(q_weight, "ctx", axis=0, tiled=True),
        lax.all_gather(k_weight, "ctx", axis=0, tiled=True),
        lax.all_gather(v_weight, "ctx", axis=0, tiled=True),
    )
    query, key, value = tuple(
        (jnp.dot(normed, weight, preferred_element_type=jnp.float32) for weight in pieces)
    )
    shard_index = lax.axis_index("ctx")
    q_pos = shard_index * tok_rows + jnp.arange(tok_rows, dtype=jnp.int32)
    positions = q_pos.astype(jnp.float32)
    q_heads = q_cols // HEAD
    kv_heads = kv_cols // HEAD
    group_size = q_heads // kv_heads
    q_rot = (
        rotate(query.reshape(tok_rows, q_heads, HEAD), positions)
        .astype(jnp.bfloat16)
        .reshape(tok_rows, kv_heads, group_size, HEAD)
    )
    k_rot = (
        rotate(key.reshape(tok_rows, kv_heads, HEAD), positions)
        .astype(jnp.bfloat16)
        .reshape(tok_rows, kv_cols)
    )
    packed = jnp.concatenate([k_rot, value.astype(jnp.bfloat16)], axis=1)
    scale = 1.0 / HEAD**0.5

    def attend(carried, kv_tile, doc_tile, hop_index):
        run_max, run_total, run_out = carried
        key_heads = kv_tile[:, :kv_cols].reshape(tok_rows, kv_heads, HEAD)
        value_heads = kv_tile[:, kv_cols:].reshape(tok_rows, kv_heads, HEAD)
        k_pos = (shard_index - hop_index) * tok_rows + jnp.arange(tok_rows, dtype=jnp.int32)
        allowed = (
            (k_pos[None, :] >= 0)
            & (k_pos[None, :] <= q_pos[:, None])
            & (doc_tile[None, :] == doc_ids[:, None])
        )
        scores = (
            jnp.einsum("tkgd,skd->kgts", q_rot, key_heads, preferred_element_type=jnp.float32)
            * scale
        )
        masked = jnp.where(allowed[None, None], scores, -1e30)
        new_max = jnp.maximum(run_max, jnp.max(masked, axis=-1))
        factor = jnp.exp(run_max - new_max)
        weights_exp = jnp.where(allowed[None, None], jnp.exp(scores - new_max[..., None]), 0.0)
        new_total = run_total * factor + jnp.sum(weights_exp, axis=-1)
        product = jnp.einsum(
            "kgts,skd->kgtd",
            weights_exp.astype(jnp.bfloat16),
            value_heads,
            preferred_element_type=jnp.float32,
        )
        return (new_max, new_total, run_out * factor[..., None] + product)

    start_state = (
        jnp.full((kv_heads, group_size, tok_rows), -1e30, jnp.float32),
        jnp.zeros((kv_heads, group_size, tok_rows), jnp.float32),
        jnp.zeros((kv_heads, group_size, tok_rows, HEAD), jnp.float32),
    )
    carried = attend(start_state, packed, doc_ids, 0)
    win_kv = packed[None]
    win_docs = doc_ids[None]
    for section_bit in range(WIN.bit_length() - 1):
        far_kv, far_docs = shifted((win_kv, win_docs), "ctx", 1 << section_bit)
        win_kv = jnp.concatenate([win_kv, far_kv], axis=0)
        win_docs = jnp.concatenate([win_docs, far_docs], axis=0)

    def scan_step(state, inputs):
        kv_tile, doc_tile, hop_index = inputs
        return (attend(state, kv_tile, doc_tile, hop_index), None)

    carried, _ = lax.scan(
        scan_step, carried, (win_kv[1:], win_docs[1:], jnp.arange(1, WIN, dtype=jnp.int32))
    )
    run_max, run_total, run_out = carried
    attended = run_out / run_total[..., None]
    attended = jnp.transpose(attended, (2, 0, 1, 3)).reshape(tok_rows, q_cols).astype(jnp.bfloat16)
    partial_terms = jnp.dot(
        attended,
        lax.all_gather(o_weight, "ctx", axis=1, tiled=True),
        preferred_element_type=jnp.float32,
    )
    return lax.psum_scatter(
        partial_terms.astype(jnp.bfloat16), "tp", scatter_dimension=1, tiled=True
    )


def solution(mesh):
    return jax.shard_map(
        local,
        mesh=mesh,
        in_specs=(
            P("ctx", "tp"),
            P("tp"),
            P("ctx"),
            P("ctx", "tp"),
            P("ctx", "tp"),
            P("ctx", "tp"),
            P("tp", "ctx"),
        ),
        out_specs=P("ctx", "tp"),
        check_vma=False,
    )
```

profile of v0, /device:TPU:0, one launch (start us, length us, event | category | flops | bytes accessed | tf_op | source)
XLA Modules:
  0.0 836.1 jit_solution(3525055102545031109)
XLA Ops:
  9.4 2.1 all_gather.19
  12.0 10.2 %all-gather.6.cloned.1.call-done = bf16[256,4096]{1,0:T(8,128)(2,1)} async-done(((bf16[256,2048]{1,0:T(8,128)(2,1)}), bf16[256,4096]{1,0:T(8,128)(2,1)}) %all-gather.6.cloned.1.call-update) | async-done | bytes 2097168 | tf_op jit(solution)/shard_map/all_gather | solution.py:36
  22.2 2.1 fusion.17
  24.3 78.0 %all-gather.8.cloned.1.call-done = bf16[4096,512]{1,0:T(8,128)(2,1)} async-done(((bf16[256,512]{1,0:T(8,128)(2,1)}), bf16[4096,512]{1,0:T(8,128)(2,1)}) %all-gather.8.cloned.1.call-update) | async-done | bytes 4194320 | tf_op jit(solution)/shard_map/all_gather | solution.py:48
  102.3 4.1 fusion.44
  107.5 72.2 %all-gather.12.cloned.1.call-done = bf16[4096,512]{1,0:T(8,128)(2,1)} async-done(((bf16[256,512]{1,0:T(8,128)(2,1)}), bf16[4096,512]{1,0:T(8,128)(2,1)}) %all-gather.12.cloned.1.call-update) | async-done | bytes 4194320 | tf_op jit(solution)/shard_map/all_gather | solution.py:49
  179.8 3.5 convolution_convert_fusion.1
  183.3 3.4 collective-permute-start.4
  186.7 17.5 %collective-permute-done.4 = bf16[1,256,1024]{2,1,0:T(8,128)(2,1)S(1)} collective-permute-done((bf16[1,256,1024]{2,1,0:T(8,128)(2,1)S(1)}, bf16[1,256,1024]{2,1,0:T(8,128)(2,1)S(1)}, u32[]{:S(2)}, u32[]{:S(2)}) %collective-permute-start.4) | collective-permute-done | bytes 524320 | tf_op jit(solution)/shard_map/ppermute | solution.py:13
  204.3 5.4 collective-permute-start.5
  209.7 17.9 %collective-permute-done.5 = bf16[2,256,1024]{2,1,0:T(8,128)(2,1)S(1)} collective-permute-done((bf16[2,256,1024]{2,1,0:T(8,128)(2,1)S(1)}, bf16[2,256,1024]{2,1,0:T(8,128)(2,1)S(1)}, u32[]{:S(2)}, u32[]{:S(2)}) %collective-permute-start.5) | collective-permute-done | bytes 1048608 | tf_op jit(solution)/shard_map/ppermute | solution.py:13
  227.8 15.3 %collective-permute-start.6 = (bf16[4,256,1024]{2,1,0:T(8,128)(2,1)S(1)}, bf16[4,256,1024]{2,1,0:T(8,128)(2,1)S(1)}, u32[]{:S(2)}, u32[]{:S(2)}) collective-permute-start(bf16[4,256,1024]{2,1,0:T(8,128)(2,1)S(1)} %pad_maximum_fusion.2), channel_id=1, source_target_pairs={{0,8},{2,10},{4,12},{6,14},{8,16},{10,18},{12,20},{14,22},{16,24},... | collective-permute-start | bytes 6291464 | tf_op jit(solution)/shard_map/ppermute | solution.py:13
  243.1 85.6 %collective-permute-done.6 = bf16[4,256,1024]{2,1,0:T(8,128)(2,1)S(1)} collective-permute-done((bf16[4,256,1024]{2,1,0:T(8,128)(2,1)S(1)}, bf16[4,256,1024]{2,1,0:T(8,128)(2,1)S(1)}, u32[]{:S(2)}, u32[]{:S(2)}) %collective-permute-start.6) | collective-permute-done | bytes 2097184 | tf_op jit(solution)/shard_map/ppermute | solution.py:13
  328.6 2.2 pad_maximum_fusion.1
  330.9 7.2 collective-permute-start.7
  338.1 3.7 collective-permute-start
  341.9 1.2 collective-permute-done
  343.1 6.6 collective-permute-start.1
  349.7 1.3 collective-permute-done.1
  351.0 173.9 %collective-permute-start.2 = (s32[4,256]{1,0:T(4,128)S(1)}, s32[4,256]{1,0:T(4,128)S(1)}, u32[]{:S(2)}, u32[]{:S(2)}) collective-permute-start(s32[4,256]{1,0:T(4,128)S(1)} %pad_add_fusion.2), channel_id=1, source_target_pairs={{0,8},{2,10},{4,12},{6,14},{8,16},{10,18},{12,20},{14,22},{16,24},... | collective-permute-start | bytes 12296 | tf_op jit(solution)/shard_map/ppermute | solution.py:13
  526.8 124.2 %collective-permute-start.3 = (s32[8,256]{1,0:T(8,128)}, s32[8,256]{1,0:T(8,128)}, u32[]{:S(2)}, u32[]{:S(2)}) collective-permute-start(s32[8,256]{1,0:T(8,128)} %pad_add_fusion.1), channel_id=1, source_target_pairs={{0,16},{2,18},{4,20},{6,22},{8,24},{10,26},{12,28},{14,30},{1,17},... | collective-permute-start | bytes 24584 | tf_op jit(solution)/shard_map/ppermute | solution.py:13
  652.0 1.3 pad_add_fusion
  653.3 1.7 reshape.263
  655.0 6.0 pad_maximum_fusion
  661.0 9.4 %convolution_bitcast_fusion = f32[32,8,16,128]{3,1,2,0:T(8,128)S(1)} fusion(bf16[4096,2048]{1,0:T(8,128)(2,1)} %all-gather.10.cloned.1.call-done, bf16[256,4096]{1,0:T(8,128)(2,1)} %all-gather.6.cloned.1.call-done, f32[4096]{0:T(1024)} %copy-done.9, f32[256]{0:T(256)S(1)} %copy-done.12), kind=kOutput, calls=%fused_computation.48 | convolution fusion | flops 4299161600 | bytes 20988928 | tf_op jit(solution)/shard_map/dot_general | solution.py:52
  675.9 1.6 fusion.31
  677.5 125.3 %while.15 = (s32[]{:T(128)}, f32[4,4,256]{2,1,0:T(4,128)S(1)}, f32[4,4,256]{2,1,0:T(4,128)S(1)}, f32[4,4,256,128]{3,2,1,0:T(8,128)S(1)}, s32[15]{0:T(128)S(1)}, ...) while((s32[]{:T(128)}, f32[4,4,256]{2,1,0:T(4,128)S(1)}, ...), condition=%wide.region_6.7_spmd.clone, body=%wide.region_3.6_spmd.clone.sunk | while | flops 549725184 | bytes 22028988 | solution.py:117
  681.1 2.1 fusion.69
  684.1 1.8 multiply_add_fusion.6
  689.4 2.1 fusion.69
  692.5 1.8 multiply_add_fusion.6
  696.4 1.1 constant_dynamic-slice_fusion.5
  697.8 2.1 fusion.69
  700.8 1.8 multiply_add_fusion.6
  706.1 2.1 fusion.69
  709.2 1.8 multiply_add_fusion.6
  713.1 1.1 constant_dynamic-slice_fusion.5
  714.5 2.1 fusion.69
  717.5 1.8 multiply_add_fusion.6
  721.5 1.1 constant_dynamic-slice_fusion.5
  722.8 2.1 fusion.69
  725.9 1.8 multiply_add_fusion.6
  731.2 2.1 fusion.69
  734.2 1.8 multiply_add_fusion.6
  739.5 2.1 fusion.69
  742.6 1.8 multiply_add_fusion.6
  747.9 2.1 fusion.69
  750.9 1.8 multiply_add_fusion.6
  756.2 2.1 fusion.69
  759.3 1.8 multiply_add_fusion.6
  764.6 2.1 fusion.69
  767.6 1.8 multiply_add_fusion.6
  773.0 2.1 fusion.69
  776.0 1.8 multiply_add_fusion.6
  781.3 2.1 fusion.69
  784.3 1.8 multiply_add_fusion.6
  789.6 2.1 fusion.69
  792.7 1.8 multiply_add_fusion.6
  798.0 2.1 fusion.69
  801.0 1.8 multiply_add_fusion.6
  802.8 1.9 copy.40
  804.7 1.8 divide_convert_fusion
  806.5 11.7 %convolution_convert_fusion = bf16[256,4096]{1,0:T(8,128)(2,1)} fusion(bf16[256,2048]{0,1:T(8,128)(2,1)S(1)} %bitcast.119, bf16[2048,4096]{1,0:T(8,128)(2,1)} %all-gather.14.cloned.1.call-done), kind=kOutput, calls=%fused_computation.27 | convolution fusion | flops 4296015872 | bytes 19922944 | tf_op jit(solution)/shard_map/dot_general | solution.py:123
  818.3 11.0 %reduce-scatter.2.cloned.1.call-done = bf16[256,2048]{1,0:T(8,128)(2,1)} async-done(((bf16[256,4096]{1,0:T(8,128)(2,1)}), bf16[256,2048]{1,0:T(8,128)(2,1)}) %reduce-scatter.2.cloned.1.call-update) | async-done | bytes 1048592 | tf_op jit(solution)/shard_map/reduce_scatter | solution.py:128
  (252 shorter events, 66.4 us)
Async XLA Ops:
  6.5 15.7 %all-gather.6.cloned.1.call-start = ((), (), s32[]{:S(2)}) async-start(), calls=%async_computation.1 | async-start | bytes 3145728 | tf_op jit(solution)/shard_map/all_gather | solution.py:36
  7.3 95.0 %all-gather.8.cloned.1.call-start = ((), (), s32[]{:S(2)}) async-start(), calls=%async_computation.2 | async-start | bytes 4456448 | tf_op jit(solution)/shard_map/all_gather | solution.py:48
  8.0 171.8 %all-gather.12.cloned.1.call-start = ((), (), s32[]{:S(2)}) async-start(), calls=%async_computation.4 | async-start | bytes 4456448 | tf_op jit(solution)/shard_map/all_gather | solution.py:49
  8.7 652.2 %all-gather.10.cloned.1.call-start = ((), (), s32[]{:S(2)}) async-start(), calls=%async_computation.3 | async-start | bytes 17825792 | tf_op jit(solution)/shard_map/all_gather | solution.py:47
  9.3 797.2 %all-gather.14.cloned.1.call-start = ((), (), s32[]{:S(2)}) async-start(), calls=%async_computation.5 | async-start | bytes 17825792 | tf_op jit(solution)/shard_map/all_gather | solution.py:125
  11.5 168.3 %copy-start.9 = (f32[4096]{0:T(1024)}, f32[4096]{0:T(1024)S(1)}, u32[]{:S(2)}) copy-start(f32[4096]{0:T(1024)S(1)} %convert_element_type.47) | copy-start | bytes 49156
  12.0 94.9 %copy-start.3 = (f32[256,64]{1,0:T(8,128)}, f32[256,64]{1,0:T(8,128)S(1)}, u32[]{:S(2)}) copy-start(f32[256,64]{1,0:T(8,128)S(1)} %get-tuple-element.151) | copy-start | bytes 196612
  24.3 82.1 %copy-start.10 = (f32[256]{0:T(256)}, f32[256]{0:T(256)S(1)}, u32[]{:S(2)}) copy-start(f32[256]{0:T(256)S(1)} %add_rsqrt_fusion) | copy-start | bytes 3076
  106.4 73.4 %copy-start.2 = (bf16[256,4096]{1,0:T(8,128)(2,1)S(1)}, bf16[256,4096]{1,0:T(8,128)(2,1)}, u32[]{:S(2)}) copy-start(bf16[256,4096]{1,0:T(8,128)(2,1)} %all-gather.6.cloned.1.call-done) | copy-start | bytes 6291460
  106.6 73.2 %copy-start.11 = (f32[256]{0:T(256)S(1)}, f32[256]{0:T(256)}, u32[]{:S(2)}) copy-start(f32[256]{0:T(256)} %copy-done.10) | copy-start | bytes 3076
  183.2 44.3 %copy-start.5 = (bf16[256,512]{1,0:T(8,128)(2,1)}, bf16[256,512]{1,0:T(8,128)(2,1)S(1)}, u32[]{:S(2)}) copy-start(bf16[256,512]{1,0:T(8,128)(2,1)S(1)} %convolution_convert_fusion.1) | copy-start | bytes 786436
  183.3 20.8 %collective-permute-start.4 = (bf16[1,256,1024]{2,1,0:T(8,128)(2,1)S(1)}, bf16[1,256,1024]{2,1,0:T(8,128)(2,1)S(1)}, u32[]{:S(2)}, u32[]{:S(2)}) collective-permute-start(bf16[1,256,1024]{2,1,0:T(8,128)(2,1)S(1)} %maximum_bitcast_fusion), channel_id=1, source_target_pairs={{0,2},{2,4},{4,6},{6,8},{8,10},{10,12},{12,14},{14,16},{16,18},{18... | collective-permute-start | bytes 1572872 | tf_op jit(solution)/shard_map/ppermute | solution.py:13
  204.2 126.7 %copy-start.1 = (bf16[1,256,1024]{2,1,0:T(8,128)(2,1)}, bf16[1,256,1024]{2,1,0:T(8,128)(2,1)S(1)}, u32[]{:S(2)}) copy-start(bf16[1,256,1024]{2,1,0:T(8,128)(2,1)S(1)} %collective-permute-done.4) | copy-start | bytes 1572868
  204.3 23.3 %collective-permute-start.5 = (bf16[2,256,1024]{2,1,0:T(8,128)(2,1)S(1)}, bf16[2,256,1024]{2,1,0:T(8,128)(2,1)S(1)}, u32[]{:S(2)}, u32[]{:S(2)}) collective-permute-start(bf16[2,256,1024]{2,1,0:T(8,128)(2,1)S(1)} %pad_maximum_fusion.4), channel_id=1, source_target_pairs={{0,4},{2,6},{4,8},{6,10},{8,12},{10,14},{12,16},{14,18},{16,20},{1... | collective-permute-start | bytes 3145736 | tf_op jit(solution)/shard_map/ppermute | solution.py:13
  227.7 110.3 %copy-start.8 = (s32[256]{0:T(256)S(1)}, s32[256]{0:T(256)}, u32[]{:S(2)}) copy-start(s32[256]{0:T(256)} %param.11) | copy-start | bytes 3076
  227.8 100.9 %collective-permute-start.6 = (bf16[4,256,1024]{2,1,0:T(8,128)(2,1)S(1)}, bf16[4,256,1024]{2,1,0:T(8,128)(2,1)S(1)}, u32[]{:S(2)}, u32[]{:S(2)}) collective-permute-start(bf16[4,256,1024]{2,1,0:T(8,128)(2,1)S(1)} %pad_maximum_fusion.2), channel_id=1, source_target_pairs={{0,8},{2,10},{4,12},{6,14},{8,16},{10,18},{12,20},{14,22},{16,24},... | collective-permute-start | bytes 6291464 | tf_op jit(solution)/shard_map/ppermute | solution.py:13
  330.9 324.1 %collective-permute-start.7 = (bf16[8,256,1024]{2,1,0:T(8,128)(2,1)}, bf16[8,256,1024]{2,1,0:T(8,128)(2,1)}, u32[]{:S(2)}, u32[]{:S(2)}) collective-permute-start(bf16[8,256,1024]{2,1,0:T(8,128)(2,1)} %pad_maximum_fusion.1), channel_id=1, source_target_pairs={{0,16},{2,18},{4,20},{6,22},{8,24},{10,26},{12,28},{14,30},{1,17},... | collective-permute-start | bytes 12582920 | tf_op jit(solution)/shard_map/ppermute | solution.py:13
  338.1 5.0 collective-permute-start
  341.8 487.4 %reduce-scatter.2.cloned.1.call-start = ((), (), s32[]{:S(2)}) async-start(), calls=%async_computation.6 | async-start | bytes 3145728 | tf_op jit(solution)/shard_map/reduce_scatter | solution.py:128
  343.1 7.9 collective-permute-start.1
  351.0 175.2 %collective-permute-start.2 = (s32[4,256]{1,0:T(4,128)S(1)}, s32[4,256]{1,0:T(4,128)S(1)}, u32[]{:S(2)}, u32[]{:S(2)}) collective-permute-start(s32[4,256]{1,0:T(4,128)S(1)} %pad_add_fusion.2), channel_id=1, source_target_pairs={{0,8},{2,10},{4,12},{6,14},{8,16},{10,18},{12,20},{14,22},{16,24},... | collective-permute-start | bytes 12296 | tf_op jit(solution)/shard_map/ppermute | solution.py:13
  526.8 125.1 %collective-permute-start.3 = (s32[8,256]{1,0:T(8,128)}, s32[8,256]{1,0:T(8,128)}, u32[]{:S(2)}, u32[]{:S(2)}) collective-permute-start(s32[8,256]{1,0:T(8,128)} %pad_add_fusion.1), channel_id=1, source_target_pairs={{0,16},{2,18},{4,20},{6,22},{8,24},{10,26},{12,28},{14,30},{1,17},... | collective-permute-start | bytes 24584 | tf_op jit(solution)/shard_map/ppermute | solution.py:13
  655.0 6.0 copy-start.12
  670.4 0.9 copy-start.4
  672.1 2.1 copy-start.6
  673.2 1.0 copy-start
  674.2 1.7 copy-start.7
  675.9 1.6 copy-start.13
Sparse Core Ops, SparseCore 0:
  8.9 13.2 all-gather.5
  25.0 77.2 all-gather.7
  105.0 74.6 all-gather.11
  182.4 326.0 all-gather.9
  511.0 292.6 all-gather.13
  818.4 10.8 reduce-scatter.1
where the time goes:
time: 839 us; the launch traced here: 836 us
  starting transfers between devices  340 us (41%)
  waiting for transfers between devices  298 us (36%)
  matrix products  89.3 us (11%)
  local copies, waits for them, and re-layouts  47.1 us (6%)
  other arithmetic  35 us (4%)
  between operations  13.8 us (2%)
  loops' own time  10.6 us (1%)
    ppermute x8, starting transfers between devices, shifted(): return lax.ppermute(block, axis, route)  340 us
    ppermute x8, waiting for transfers between devices, shifted(): return lax.ppermute(block, axis, route)  124 us
    all_gather x1, waiting for transfers between devices, local(): lax.all_gather(k_weight, 'ctx', axis=0, tiled=True)  78 us
    all_gather x1, waiting for transfers between devices, local(): lax.all_gather(v_weight, 'ctx', axis=0, tiled=True)  72.2 us
    dynamic_slice x60, local copies, waits for them, and re-layouts, local(): lax.scan(scan_step, carried, (win_kv[1:], win_docs[1:], jnp.arange(1, WIN...  39.7 us
    dot_general x16, matrix products, attend(): jnp.einsum('tkgd,skd->kgts', q_rot, key_heads, preferred_element_type=jnp...  32.4 us
    dot_general x16, matrix products, attend(): jnp.einsum('kgts,skd->kgtd', weights_exp.astype(jnp.bfloat16), value_head...  28.2 us
    dot_general x3, matrix products, local(): jnp.dot(normed, weight, preferred_element_type=jnp.float32)  17 us
  transfers between devices with their start and end apart: 14, of which 11 were waited for; matrix products, arithmetic and copies ran while one was open for 19% of the time, Pallas kernels for 0%

commit v1 on v0

v1 whole, which is shorter than its diff:
```python
import functools
import math
import jax
import jax.numpy as jnp
from jax import lax
from jax.experimental import pallas as pl
from jax.experimental.pallas import tpu as pltpu
from jax.sharding import Mesh, PartitionSpec as P

HEAD = 128


def rotate(values, positions):
    half_dim = values.shape[-1] // 2
    inv_freq = 500000.0 ** (-(jnp.arange(half_dim, dtype=jnp.float32) * 2.0) / values.shape[-1])
    angles = positions[:, None] * inv_freq[None, :]
    cos_part = jnp.cos(angles)[:, None, :]
    sin_part = jnp.sin(angles)[:, None, :]
    first_half = values[..., :half_dim]
    second_half = values[..., half_dim:]
    return jnp.concatenate(
        [
            first_half * cos_part - second_half * sin_part,
            second_half * cos_part + first_half * sin_part,
        ],
        axis=-1,
    )


def flash_kernel(
    kv_heads, group, chunk, n_b, lo_ref, b_ref, q_ref, kv_ref, docq_ref, dock_ref, out_ref, m_ref, l_ref, acc_ref
):
    rows = q_ref.shape[0]
    tile = pl.program_id(0)
    shard = tile * n_b + b_ref[0]
    first_row = shard * rows
    hi = (first_row + rows - 1) // chunk
    lo = lo_ref[tile]
    scale2 = math.log2(math.e) / math.sqrt(HEAD)
    q_pos = first_row + lax.broadcasted_iota(jnp.int32, (rows, chunk), 0)
    k_rel = lax.broadcasted_iota(jnp.int32, (rows, chunk), 1)
    docq = docq_ref[...]

    def step(c, first):
        start = pl.multiple_of(c * chunk, chunk)
        keys = pl.ds(start, chunk)
        allowed = (k_rel + start <= q_pos) & (dock_ref[:, keys] == docq)
        for kh in range(kv_heads):
            k = kv_ref[keys, kh * HEAD : (kh + 1) * HEAD]
            v = kv_ref[keys, (kv_heads + kh) * HEAD : (kv_heads + kh + 1) * HEAD]
            for g in range(group):
                h = kh * group + g
                q = q_ref[:, h * HEAD : (h + 1) * HEAD]
                s = lax.dot_general(q, k, (((1,), (1,)), ((), ())), preferred_element_type=jnp.float32)
                s = jnp.where(allowed, s * scale2, -1e30)
                top = jnp.max(s, axis=-1, keepdims=True)
                if first:
                    new = top
                else:
                    old = m_ref[h]
                    new = jnp.maximum(old, top)
                e = jnp.exp2(s - new)
                total = jnp.sum(e, axis=-1, keepdims=True)
                prod = jnp.dot(e.astype(jnp.bfloat16), v, preferred_element_type=jnp.float32)
                m_ref[h] = new
                if first:
                    l_ref[h] = total
                    acc_ref[h] = prod
                else:
                    factor = jnp.exp2(old - new)
                    l_ref[h] = l_ref[h] * factor + total
                    acc_ref[h] = acc_ref[h] * factor + prod

    step(hi, True)

    def body(i, _):
        step(hi - 1 - i, False)
        return 0

    lax.fori_loop(0, hi - lo, body, 0)
    for h in range(kv_heads * group):
        out_ref[:, h * HEAD : (h + 1) * HEAD] = (acc_ref[h] / l_ref[h]).astype(jnp.bfloat16)


def flash(q, kv, docq, docs, lo, b, n_a, n_b, kv_heads, group, chunk):
    rows = q.shape[0] // n_a
    heads = kv_heads * group
    keys = kv.shape[0]
    smem = pl.BlockSpec(memory_space=pltpu.SMEM)
    return pl.pallas_call(
        functools.partial(flash_kernel, kv_heads, group, chunk, n_b),
        grid=(n_a,),
        out_shape=jax.ShapeDtypeStruct(q.shape, jnp.bfloat16),
        in_specs=[
            smem,
            smem,
            pl.BlockSpec((rows, heads * HEAD), lambda i: (i, 0)),
            pl.BlockSpec((keys, kv.shape[1]), lambda i: (0, 0)),
            pl.BlockSpec((rows, 1), lambda i: (i, 0)),
            pl.BlockSpec((1, keys), lambda i: (0, 0)),
        ],
        out_specs=pl.BlockSpec((rows, heads * HEAD), lambda i: (i, 0)),
        scratch_shapes=[
            pltpu.VMEM((heads, rows, 1), jnp.float32),
            pltpu.VMEM((heads, rows, 1), jnp.float32),
            pltpu.VMEM((heads, rows, HEAD), jnp.float32),
        ],
        compiler_params=pltpu.CompilerParams(vmem_limit_bytes=40 << 20),
    )(lo, b, q, kv, docq, docs)


def local(n_a, n_b, tokens, norm_gain, doc_ids, q_weight, k_weight, v_weight, o_weight):
    t = tokens.shape[0]
    q_cols, kv_cols = q_weight.shape[1] // n_a, k_weight.shape[1] // n_a
    kv_heads = kv_cols // HEAD
    group = q_cols // kv_cols
    cols = q_cols + 2 * kv_cols
    b = lax.axis_index("b")

    w_local = jnp.concatenate(
        [w.reshape(t if w.shape[0] == t else w.shape[0], n_a, -1) for w in (q_weight, k_weight, v_weight)], axis=2
    ).transpose(1, 0, 2)
    w_rows = w_local.shape[1]
    part = lax.all_to_all(w_local, "a", 0, 0) if n_a > 1 else w_local
    weight = lax.all_gather(part, "b", axis=1).reshape(n_a * n_b * w_rows, cols)

    half = lax.all_gather(tokens, "a", axis=0, tiled=True)
    whole = lax.all_gather(half, "tp", axis=1, tiled=True)
    gain_whole = lax.all_gather(norm_gain, "tp", axis=0, tiled=True)
    docs = lax.all_gather(doc_ids, ("a", "b"), axis=0, tiled=True)

    x_float = whole.astype(jnp.float32)
    mean_sq = jnp.mean(x_float * x_float, axis=-1, keepdims=True)
    normed = (x_float * lax.rsqrt(mean_sq + 1e-05) * gain_whole.astype(jnp.float32)).astype(jnp.bfloat16)
    qkv = jnp.dot(normed, weight, preferred_element_type=jnp.float32)

    rows = n_a * t
    pos = ((jnp.arange(n_a, dtype=jnp.int32) * n_b + b)[:, None] * t + jnp.arange(t, dtype=jnp.int32)[None]).reshape(rows)
    rot = rotate(qkv[:, : q_cols + kv_cols].reshape(rows, -1, HEAD), pos.astype(jnp.float32))
    rot = rot.astype(jnp.bfloat16).reshape(rows, q_cols + kv_cols)
    q_rot = rot[:, :q_cols]
    kv = jnp.concatenate([rot[:, q_cols:], qkv[:, q_cols + kv_cols :].astype(jnp.bfloat16)], axis=1)
    kv = lax.all_gather(kv.reshape(n_a, t, 2 * kv_cols), "b", axis=1).reshape(n_a * n_b * t, 2 * kv_cols)

    docq = lax.dynamic_index_in_dim(docs.reshape(n_a, n_b, t), b, 1, keepdims=False)
    chunk = t * min(4, n_a * n_b)
    lo = jnp.sum((docs[None, :] < docq[:, :1]).astype(jnp.int32), axis=1) // chunk
    attended = flash(
        q_rot, kv, docq.reshape(rows, 1), docs[None], lo, b.astype(jnp.int32)[None], n_a, n_b, kv_heads, group, chunk
    )

    o_whole = lax.all_gather(o_weight, "b", axis=1, tiled=True)
    att_whole = lax.all_gather(attended, "a", axis=1, tiled=True)
    partial = jnp.dot(att_whole, o_whole, preferred_element_type=jnp.float32).astype(jnp.bfloat16)
    if n_a > 1:
        partial = lax.all_to_all(partial.reshape(n_a, t, -1), "a", 0, 0).transpose(1, 0, 2).reshape(t, -1)
    return lax.psum_scatter(partial, "tp", scatter_dimension=1, tiled=True)


def solution(mesh):
    n_ctx, n_tp = mesh.shape["ctx"], mesh.shape["tp"]

    def run(tokens, norm_gain, doc_ids, q_weight, k_weight, v_weight, o_weight):
        n_a = math.gcd(math.gcd(k_weight.shape[1] // n_tp // HEAD, n_ctx), 4)
        n_b = n_ctx // n_a
        grid = Mesh(mesh.devices.reshape(n_a, n_b, n_tp), ("a", "b", "tp"))
        ctx = ("a", "b")
        return jax.shard_map(
            functools.partial(local, n_a, n_b),
            mesh=grid,
            in_specs=(P(ctx, "tp"), P("tp"), P(ctx), P(ctx, "tp"), P(ctx, "tp"), P(ctx, "tp"), P("tp", ctx)),
            out_specs=P(ctx, "tp"),
            check_vma=False,
        )(tokens, norm_gain, doc_ids, q_weight, k_weight, v_weight, o_weight)

    return run
```

time: 839 us -> 482 us (0.57)
  starting transfers between devices: 340 us -> 0.24 us
  blocking collectives: 2.08 us -> 178 us
  waiting for transfers between devices: 298 us -> 219 us
  matrix products: 89.3 us -> 17.4 us
  local copies, waits for them, and re-layouts: 47.1 us -> 18.4 us
  other arithmetic: 35 us -> 7.27 us
  Pallas kernels: 0 us -> 27.2 us
  loops' own time: 10.6 us -> 0 us
    ppermute x8 -> x0, starting transfers between devices: 340 us -> none  [shifted(): return lax.ppermute(block, axis, route)]
    all_to_all x0 -> x2, blocking collectives: none -> 135 us  [the longest x1 84.4 us: local(): part = lax.all_to_all(w_local, 'a', 0, 0) if n_a > 1 else w_local]
    ppermute x8 -> x0, waiting for transfers between devices: 124 us -> none  [shifted(): return lax.ppermute(block, axis, route)]
    dot_general x36 -> x2, matrix products: 89.3 us -> 17.4 us  [the longest x1 9.5 us: local(): qkv = jnp.dot(normed, weight, preferred_element_type=jnp.float32)]
    all_gather x5 -> x6, waiting for transfers between devices: 160 us -> 208 us  [the longest x1 82.2 us: local(): att_whole = lax.all_gather(attended, 'a', axis=1, tiled=True)]
    all_gather x1 -> x2, blocking collectives: 2.08 us -> 42.9 us  [the longest x1 41.1 us: local(): docs = lax.all_gather(doc_ids, ('a', 'b'), axis=0, tiled=True)]
    dynamic_slice x60 -> x1, local copies, waits for them, and re-layouts: 39.7 us -> 0.01 us  [local(): lax.dynamic_index_in_dim(docs.reshape(n_a, n_b, t), b, 1, keepdims=False)]
    pallas_call x0 -> x1, Pallas kernels: none -> 27.2 us  [flash(): pl.pallas_call(functools.partial(flash_kernel, kv_heads, group, chunk, n_...]
  transfers between devices with their start and end apart: 14 -> 7, of which waited for: 11 -> 6; matrix products, arithmetic and copies ran while one was open for 19% -> 3% of each run, Pallas kernels for 0% -> 6%
where the time goes in v1:
time: 482 us; the launch traced here: 481 us
  waiting for transfers between devices  219 us (45%)
  blocking collectives  178 us (37%)
  Pallas kernels  27.2 us (6%)
  local copies, waits for them, and re-layouts  18.4 us (4%)
  matrix products  17.4 us (4%)
  between operations  13.7 us (3%)
  other arithmetic  7.27 us (2%)
    all_to_all x1, blocking collectives, local(): part = lax.all_to_all(w_local, 'a', 0, 0) if n_a > 1 else w_local  84.4 us
    all_gather x1, waiting for transfers between devices, local(): att_whole = lax.all_gather(attended, 'a', axis=1, tiled=True)  82.2 us
    all_gather x1, waiting for transfers between devices, local(): weight = lax.all_gather(part, 'b', axis=1).reshape(n_a * n_b * w_rows, cols)  68 us
    all_to_all x1, blocking collectives, local(): lax.all_to_all(partial.reshape(n_a, t, -1), 'a', 0, 0).transpose(1, 0, 2)  51 us
    all_gather x1, blocking collectives, local(): docs = lax.all_gather(doc_ids, ('a', 'b'), axis=0, tiled=True)  41.1 us
    pallas_call x1, Pallas kernels, flash(): pl.pallas_call(functools.partial(flash_kernel, kv_heads, group, chunk, n_...  27.2 us
    all_gather x1, waiting for transfers between devices, local(): half = lax.all_gather(tokens, 'a', axis=0, tiled=True)  26.4 us
    all_gather x1, waiting for transfers between devices, local(): o_whole = lax.all_gather(o_weight, 'b', axis=1, tiled=True)  19.1 us
  transfers between devices with their start and end apart: 7, of which 6 were waited for; matrix products, arithmetic and copies ran while one was open for 3% of the time, Pallas kernels for 6%

profile of v1, /device:TPU:0, one launch (start us, length us, event | category | flops | bytes accessed | tf_op | source)
XLA Modules:
  0.0 481.0 jit_solution(2834917586646144945)
XLA Ops:
  6.5 0.0 all-gather.9.cloned.1.call-start
  6.5 0.7 all-gather.9.cloned.1.call-update
  7.3 0.0 all-gather.19.cloned.1.call-start
  7.3 1.1 copy.45
  8.4 1.1 copy.44
  9.5 1.5 copy.43
  11.0 0.1 maximum_bitcast_fusion
  11.1 84.4 %all_to_all.10 = bf16[4,256,768]{1,2,0:T(8,128)(2,1)} all-to-all(bf16[4,256,768]{1,2,0:T(8,128)(2,1)S(1)} %maximum_bitcast_fusion), channel_id=1, replica_groups=mesh['a'=4,'b'=4,'tp'=2] {'a'}, dimensions={0} | all-to-all | bytes 3145728 | tf_op jit(solution)/shard_map/all_to_all | solution.py:124
  95.5 0.0 copy-start.2
  95.5 0.0 all-gather.19.cloned.1.call-update
  95.5 0.0 all-gather.11.cloned.1.call-start
  95.5 26.4 %all-gather.9.cloned.1.call-done = bf16[1024,2048]{1,0:T(8,128)(2,1)} async-done(((bf16[256,2048]{1,0:T(8,128)(2,1)}), bf16[1024,2048]{1,0:T(8,128)(2,1)}) %all-gather.9.cloned.1.call-update) | async-done | bytes 4194320 | tf_op jit(solution)/shard_map/all_gather | solution.py:127
  121.9 0.0 all-gather.11.cloned.1.call-update
  122.0 0.0 all-gather.13.cloned.1.call-start
  122.0 0.0 copy-done.2
  122.0 1.8 all_gather.30
  123.8 0.1 convert_bitcast_fusion
  123.9 1.0 multiply_cosine_fusion
  124.9 68.0 %all-gather.19.cloned.1.call-done = bf16[4,1024,768]{1,2,0:T(8,128)(2,1)} async-done(((bf16[4,256,768]{1,2,0:T(8,128)(2,1)}), bf16[4,1024,768]{1,2,0:T(8,128)(2,1)}) %all-gather.19.cloned.1.call-update) | async-done | bytes 6291472 | tf_op jit(solution)/shard_map/all_gather | solution.py:125
  192.9 8.8 %copy.46 = bf16[4,1024,768]{2,1,0:T(8,128)(2,1)} copy(bf16[4,1024,768]{1,2,0:T(8,128)(2,1)} %all-gather.19.cloned.1.call-done) | data formatting | bytes 12582912 | tf_op jit(solution)/shard_map/all_gather | solution.py:125
  201.7 12.7 %all-gather.11.cloned.1.call-done = bf16[1024,4096]{1,0:T(8,128)(2,1)} async-done(((bf16[1024,2048]{1,0:T(8,128)(2,1)}), bf16[1024,4096]{1,0:T(8,128)(2,1)}) %all-gather.11.cloned.1.call-update) | async-done | bytes 8388624 | tf_op jit(solution)/shard_map/all_gather | solution.py:128
  214.4 0.0 copy-start.1
  214.4 5.2 %fusion = f32[1024]{0:T(1024)S(1)} fusion(bf16[1024,4096]{1,0:T(8,128)(2,1)} %all-gather.11.cloned.1.call-done), kind=kLoop, calls=%fused_computation.2 | loop fusion | flops 12581888 | bytes 8392704 | tf_op jit(solution)/shard_map/reduce_sum | solution.py:133
  219.6 0.5 copy-done.1
  220.2 9.5 %fusion.3 = f32[1024,768]{0,1:T(8,128)S(1)} fusion(bf16[4096,768]{1,0:T(8,128)(2,1)} %bitcast.34, bf16[1024,4096]{1,0:T(8,128)(2,1)S(1)} %copy-done.1, f32[4096]{0:T(1024)S(1)} %convert_element_type.33, f32[1024]{0:T(1024)S(1)} %add_rsqrt_fusion), kind=kOutput, calls=%fused_computation.5 | convolution fusion | flops 6459228160 | bytes 17846272 | tf_op jit(solution)/shard_map/dot_general | solution.py:135
  229.7 0.3 slice.30
  230.0 0.4 subtract_convert_fusion
  230.5 0.0 copy-start.3
  230.5 0.1 pad_maximum_fusion
  230.7 1.0 copy.51
  231.7 0.0 all-gather.13.cloned.1.call-update
  231.7 0.0 all-gather.17.cloned.1.call-start
  231.7 0.5 all-gather.17.cloned.1.call-update
  232.3 0.0 all-gather.15.cloned.1.call-start
  232.3 0.0 copy-done.3
  232.3 41.1 %all-gather.1 = s32[16,1,256]{2,1,0:T(1,128)S(1)} all-gather(s32[1,1,256]{2,1,0:T(1,128)S(1)} %bitcast.45), channel_id=1, replica_groups=mesh['a'=4,'b'=4,'tp'=2] {'a','b'}, dimensions={0}, use_global_device_ids=true | all-gather | bytes 17408 | tf_op jit(solution)/shard_map/all_gather | solution.py:130
  273.5 0.2 copy.49.docq_ref
  273.7 0.1 slice_reduce_fusion
  273.9 0.2 convert_reduce_fusion
  274.1 0.1 slice.33
  274.2 0.5 copy.54.q_ref
  274.7 0.0 all-gather.13.cloned.1.call-done
  274.7 0.0 copy-start
  274.8 1.6 copy-done
  276.3 27.2 %shard_map.73 = bf16[1024,512]{1,0:T(8,128)(2,1)} custom-call(s32[4]{0:T(128)S(1)} %and_select_fusion.lo_ref, s32[1]{0:T(128)} %bitcast.2.b_ref, bf16[1024,512]{1,0:T(8,128)(2,1)S(1)} %copy.54.q_ref, bf16[4096,256]{1,0:T(8,128)(2,1)S(1)} %bitcast.28, s32[1024,1]{1,0:T(8,128)S(1)} %copy.49.docq_ref, s32[1,4096]{1,0:T(1,128)S(1)} %bitcast.30), custom_call_target="tpu_custom_call" | custom-call | tf_op jit(solution)/shard_map/pallas_call | solution.py:90
  303.6 0.0 all-gather.15.cloned.1.call-update
  303.6 0.0 reduce-scatter.2.cloned.1.call-start
  303.6 19.1 %all-gather.17.cloned.1.call-done = bf16[2048,1024]{1,0:T(8,128)(2,1)} async-done(((bf16[2048,256]{1,0:T(8,128)(2,1)}), bf16[2048,1024]{1,0:T(8,128)(2,1)}) %all-gather.17.cloned.1.call-update) | async-done | bytes 4194320 | tf_op jit(solution)/shard_map/all_gather | solution.py:152
  322.7 82.2 %all-gather.15.cloned.1.call-done = bf16[1024,2048]{1,0:T(8,128)(2,1)} async-done(((bf16[1024,512]{1,0:T(8,128)(2,1)}), bf16[1024,2048]{1,0:T(8,128)(2,1)}) %all-gather.15.cloned.1.call-update) | async-done | bytes 4194320 | tf_op jit(solution)/shard_map/all_gather | solution.py:153
  404.9 8.0 %convolution_convert_fusion = bf16[1024,1024]{1,0:T(8,128)(2,1)S(1)} fusion(bf16[1024,2048]{1,0:T(8,128)(2,1)} %all-gather.15.cloned.1.call-done, bf16[2048,1024]{1,0:T(8,128)(2,1)} %all-gather.17.cloned.1.call-done), kind=kOutput, calls=%fused_computation.8 | convolution fusion | flops 4296015872 | bytes 10485760 | tf_op jit(solution)/shard_map/dot_general | solution.py:154
  412.9 51.0 %all_to_all.11 = bf16[4,256,1024]{2,1,0:T(8,128)(2,1)S(1)} all-to-all(bf16[4,256,1024]{2,1,0:T(8,128)(2,1)S(1)} %bitcast.38), channel_id=1, replica_groups=mesh['a'=4,'b'=4,'tp'=2] {'a'}, dimensions={0} | all-to-all | bytes 4194304 | tf_op jit(solution)/shard_map/all_to_all | solution.py:156
  463.9 1.5 copy.55
  465.4 0.0 reduce-scatter.2.cloned.1.call-update
  465.4 8.8 %reduce-scatter.2.cloned.1.call-done = bf16[256,2048]{1,0:T(8,128)(2,1)} async-done(((bf16[256,4096]{1,0:T(8,128)(2,1)}), bf16[256,2048]{1,0:T(8,128)(2,1)}) %reduce-scatter.2.cloned.1.call-update) | async-done | bytes 1048592 | tf_op jit(solution)/shard_map/reduce_scatter | solution.py:157
  (13 shorter events, 0.2 us)
Async XLA Ops:
  6.5 115.4 %all-gather.9.cloned.1.call-start = ((), (), s32[]{:S(2)}) async-start(), calls=%async_computation.3 | async-start | bytes 5242880 | tf_op jit(solution)/shard_map/all_gather | solution.py:127
  7.3 185.7 %all-gather.19.cloned.1.call-start = ((), (), s32[]{:S(2)}) async-start(), calls=%async_computation.9 | async-start | bytes 7864320 | tf_op jit(solution)/shard_map/all_gather | solution.py:125
  95.5 26.6 %copy-start.2 = (bf16[2048]{0:T(1024)(128)(2,1)S(1)}, bf16[2048]{0:T(1024)(128)(2,1)}, u32[]{:S(2)}) copy-start(bf16[2048]{0:T(1024)(128)(2,1)} %param.8) | copy-start | bytes 12292
  95.5 118.9 %all-gather.11.cloned.1.call-start = ((), (), s32[]{:S(2)}) async-start(), calls=%async_computation.4 | async-start | bytes 12582912 | tf_op jit(solution)/shard_map/all_gather | solution.py:128
  122.0 152.8 %all-gather.13.cloned.1.call-start = ((), (), s32[]{:S(2)}) async-start(), calls=%async_computation.5 | async-start | bytes 2621440 | tf_op jit(solution)/shard_map/all_gather | solution.py:143
  214.4 5.8 %copy-start.1 = (bf16[1024,4096]{1,0:T(8,128)(2,1)S(1)}, bf16[1024,4096]{1,0:T(8,128)(2,1)}, u32[]{:S(2)}) copy-start(bf16[1024,4096]{1,0:T(8,128)(2,1)} %all-gather.11.cloned.1.call-done) | copy-start | bytes 25165828
  230.5 1.9 copy-start.3
  231.7 91.0 %all-gather.17.cloned.1.call-start = ((), (), s32[]{:S(2)}) async-start(), calls=%async_computation.7 | async-start | bytes 5242880 | tf_op jit(solution)/shard_map/all_gather | solution.py:152
  232.3 172.7 %all-gather.15.cloned.1.call-start = ((), (), s32[]{:S(2)}) async-start(), calls=%async_computation.6 | async-start | bytes 5242880 | tf_op jit(solution)/shard_map/all_gather | solution.py:153
  274.7 1.6 copy-start
  303.6 170.6 %reduce-scatter.2.cloned.1.call-start = ((), (), s32[]{:S(2)}) async-start(), calls=%async_computation.8 | async-start | bytes 3145728 | tf_op jit(solution)/shard_map/reduce_scatter | solution.py:157
Sparse Core Ops, SparseCore 0:
  8.9 112.9 all-gather.8
  123.8 69.1 all-gather.18
  194.5 19.8 all-gather.10
  231.8 36.5 all-gather.12
  270.1 52.5 all-gather.16
  324.1 80.7 all-gather.14
  465.5 8.6 reduce-scatter.1

commit v2 on v1

--- a/solution.py
+++ b/solution.py
@@ -109,6 +109,308 @@
     )(lo, b, q, kv, docq, docs)
 
 
+MESH = pl.DeviceIdType.MESH
+
+
+def place(n, axis, offset):
+    return lax.rem(lax.axis_index(axis) + offset, n)
+
+
+def greet(sizes):
+    barrier = pltpu.get_barrier_semaphore()
+    count = 0
+    for axis, n in sizes.items():
+        for o in range(1, n):
+            pl.semaphore_signal(barrier, inc=1, device_id={axis: place(n, axis, o)}, device_id_type=MESH)
+            count += 1
+    pl.semaphore_wait(barrier, count)
+
+
+def push(src, dst, send, recv, axis, index):
+    return pltpu.make_async_remote_copy(
+        src_ref=src, dst_ref=dst, send_sem=send, recv_sem=recv, device_id={axis: index}, device_id_type=MESH
+    )
+
+
+def line(n, own, spot, right_sem, left_sem, recv_sem, handle):
+    me = lax.axis_index("a")
+    right, left = lax.rem(me + 1, n), lax.rem(me + n - 1, n)
+
+    def to_right(k, src, index):
+        return push(src, spot(index), right_sem.at[k], recv_sem.at[index], "a", right)
+
+    def to_left(k, src, index):
+        return push(src, spot(index), left_sem.at[k], recv_sem.at[index], "a", left)
+
+    def begin():
+        @pl.when(me < n - 1)
+        def _():
+            to_right(0, own, me).start()
+
+        @pl.when(me > 0)
+        def _():
+            to_left(0, own, me).start()
+
+    def step(k):
+        @pl.when(me >= k)
+        def _():
+            index = me - k
+            to_left(k, spot(index), index).wait_recv()
+
+            @pl.when(me < n - 1)
+            def _():
+                to_right(k, spot(index), index).start()
+
+            handle(k, 0, index)
+
+        @pl.when(me + k < n)
+        def _():
+            index = me + k
+            to_right(k, spot(index), index).wait_recv()
+
+            @pl.when(me > 0)
+            def _():
+                to_left(k, spot(index), index).start()
+
+            handle(k, 1, index)
+
+    def end():
+        for k in range(n):
+            @pl.when((me >= k) & (me < n - 1))
+            def _():
+                to_right(k, own if k == 0 else spot(me - k), me - k).wait_send()
+
+            @pl.when((me + k < n) & (me > 0))
+            def _():
+                to_left(k, own if k == 0 else spot(me + k), me + k).wait_send()
+
+    return begin, step, end
+
+
+def input_kernel(
+    n_a, n_b, w_ref, tok_ref, gain_ref, weight_ref, whole_ref, gain_out,
+    own_sem, z_send, z_recv, p_send, p_recv, right_sem, left_sem, t_recv, c_send, c_recv, g_send, g_recv,
+):
+    a, b, c = lax.axis_index("a"), lax.axis_index("b"), lax.axis_index("tp")
+    t, width = tok_ref.shape
+    other = 1 - c
+    greet({"a": n_a, "b": n_b, "tp": 2})
+
+    def spot(index, core=c):
+        return whole_ref.at[
+            pl.ds(pl.multiple_of(index * t, t), t), pl.ds(pl.multiple_of(core * width, width), width)
+        ]
+
+    def gain_spot(core):
+        return gain_out.at[:, pl.ds(pl.multiple_of(core * width, width), width)]
+
+    exchange = []
+    for o in range(1, n_a):
+        to = place(n_a, "a", o)
+        exchange.append(push(w_ref.at[to], weight_ref.at[a, b], z_send.at[o - 1], z_recv.at[a], "a", to))
+        exchange[-1].start()
+
+    def cross(k, side, index):
+        src = tok_ref if k == 0 else spot(index)
+        return push(src, spot(index), c_send.at[index], c_recv.at[index], "tp", other)
+
+    begin, step, end = line(
+        n_a, tok_ref, spot, right_sem, left_sem, t_recv, lambda k, side, index: cross(k, side, index).start()
+    )
+    begin()
+
+    def plane(k, o):
+        index = place(n_a, "a", k)
+        src = w_ref.at[index] if k == 0 else weight_ref.at[index, b]
+        return push(
+            src, weight_ref.at[index, b], p_send.at[k, o - 1], p_recv.at[index, b], "b", place(n_b, "b", o)
+        )
+
+    for o in range(1, n_b):
+        plane(0, o).start()
+    cross(0, 0, a).start()
+    gain = push(gain_ref, gain_spot(c), g_send, g_recv, "tp", other)
+    gain.start()
+    own = [
+        pltpu.make_async_copy(w_ref.at[a], weight_ref.at[a, b], own_sem.at[0]),
+        pltpu.make_async_copy(tok_ref, spot(a), own_sem.at[1]),
+        pltpu.make_async_copy(gain_ref, gain_spot(c), own_sem.at[2]),
+    ]
+    for copy in own:
+        copy.start()
+    for k in range(1, n_a):
+        index = place(n_a, "a", k)
+        push(
+            w_ref.at[index], weight_ref.at[index, b], z_send.at[k - 1], z_recv.at[index], "a", index
+        ).wait_recv()
+        for o in range(1, n_b):
+            plane(k, o).start()
+        step(k)
+    for k in range(n_a):
+        for o in range(1, n_b):
+            index, source = place(n_a, "a", k), place(n_b, "b", o)
+            push(
+                w_ref.at[index], weight_ref.at[index, source], p_send.at[k, o - 1], p_recv.at[index, source], "b", source
+            ).wait_recv()
+    for index in range(n_a):
+        push(spot(index), spot(index, other), c_send.at[index], c_recv.at[index], "tp", other).wait_recv()
+    push(gain_ref, gain_spot(other), g_send, g_recv, "tp", other).wait_recv()
+    for copy in exchange:
+        copy.wait_send()
+    for k in range(n_a):
+        for o in range(1, n_b):
+            plane(k, o).wait_send()
+    for index in range(n_a):
+        push(spot(index), spot(index), c_send.at[index], c_recv.at[index], "tp", other).wait_send()
+    gain.wait_send()
+    end()
+    for copy in own:
+        copy.wait()
+
+
+def kv_kernel(n_b, kv_ref, out_ref, own_sem, send, recv):
+    b = lax.axis_index("b")
+    greet({"b": n_b})
+    copies = [
+        push(kv_ref, out_ref.at[:, b], send.at[o - 1], recv.at[b], "b", place(n_b, "b", o)) for o in range(1, n_b)
+    ]
+    for copy in copies:
+        copy.start()
+    own = pltpu.make_async_copy(kv_ref, out_ref.at[:, b], own_sem)
+    own.start()
+    for o in range(1, n_b):
+        source = place(n_b, "b", o)
+        push(kv_ref, out_ref.at[:, source], send.at[o - 1], recv.at[source], "b", source).wait_recv()
+    for copy in copies:
+        copy.wait_send()
+    own.wait()
+
+
+def wide_kernel(n_a, n_b, att_ref, o_ref, att_out, o_out, own_sem, right_sem, left_sem, t_recv, send, recv):
+    a, b = lax.axis_index("a"), lax.axis_index("b")
+    greet({"a": n_a, "b": n_b})
+    width, o_width = att_ref.shape[1], o_ref.shape[1]
+
+    def spot(index):
+        return att_out.at[:, pl.ds(pl.multiple_of(index * width, width), width)]
+
+    def o_spot(index):
+        return o_out.at[:, pl.ds(pl.multiple_of(index * o_width, o_width), o_width)]
+
+    begin, step, end = line(n_a, att_ref, spot, right_sem, left_sem, t_recv, lambda k, side, index: None)
+    begin()
+    copies = [
+        push(o_ref, o_spot(b), send.at[o - 1], recv.at[b], "b", place(n_b, "b", o)) for o in range(1, n_b)
+    ]
+    for copy in copies:
+        copy.start()
+    own = [
+        pltpu.make_async_copy(att_ref, spot(a), own_sem.at[0]),
+        pltpu.make_async_copy(o_ref, o_spot(b), own_sem.at[1]),
+    ]
+    for copy in own:
+        copy.start()
+    for k in range(1, n_a):
+        step(k)
+    for o in range(1, n_b):
+        source = place(n_b, "b", o)
+        push(o_ref, o_spot(source), send.at[o - 1], recv.at[source], "b", source).wait_recv()
+    for copy in copies:
+        copy.wait_send()
+    end()
+    for copy in own:
+        copy.wait()
+
+
+def final_kernel(
+    n_a, part_ref, out_ref, got_ref, sum_ref, x_send, x_recv, o_send, o_recv, own_sem
+):
+    a, b, c = lax.axis_index("a"), lax.axis_index("b"), lax.axis_index("tp")
+    half = n_a // 2
+    w = part_ref.shape[2]
+    barrier = pltpu.get_barrier_semaphore()
+    for o in range(n_a):
+        for core in (c, 1 - c) if o else (1 - c,):
+            pl.semaphore_signal(
+                barrier, inc=1, device_id={"a": place(n_a, "a", o), "tp": core}, device_id_type=MESH
+            )
+    pl.semaphore_wait(barrier, 2 * n_a - 1)
+    swaps = [
+        push(part_ref.at[(1 - c) * half + i], got_ref.at[i], x_send.at[i], x_recv.at[i], "tp", 1 - c)
+        for i in range(half)
+    ]
+    for copy in swaps:
+        copy.start()
+    column = lax.rem(a, half)
+    goal_core = a // half
+
+    def spot(index):
+        return out_ref.at[:, pl.ds(pl.multiple_of(index * w, w), w)]
+
+    def away(i):
+        return pltpu.make_async_remote_copy(
+            src_ref=sum_ref.at[i], dst_ref=spot(column), send_sem=o_send.at[i], recv_sem=o_recv.at[column],
+            device_id={"a": c * half + i, "tp": goal_core}, device_id_type=MESH,
+        )
+
+    def home(i):
+        return pltpu.make_async_copy(sum_ref.at[i], spot(column), own_sem)
+
+    for i in range(half):
+        swaps[i].wait_recv()
+        mine = part_ref[c * half + i].astype(jnp.float32)
+        sum_ref[i] = (mine + got_ref[i].astype(jnp.float32)).astype(jnp.bfloat16)
+        is_me = (c * half + i == a) & (goal_core == c)
+
+        @pl.when(jnp.logical_not(is_me))
+        def _():
+            away(i).start()
+
+        @pl.when(is_me)
+        def _():
+            home(i).start()
+
+    for i in range(half):
+        is_me = (c * half + i == a) & (goal_core == c)
+
+        @pl.when(jnp.logical_not(is_me))
+        def _():
+            away(i).wait_send()
+
+        @pl.when(is_me)
+        def _():
+            home(i).wait()
+
+    for j in range(half):
+        @pl.when(jnp.logical_not((c * half + j == a) & (goal_core == c)))
+        def _():
+            pltpu.make_async_remote_copy(
+                src_ref=sum_ref.at[0], dst_ref=spot(j), send_sem=o_send.at[0], recv_sem=o_recv.at[j],
+                device_id={"a": place(n_a, "a", 1)}, device_id_type=MESH,
+            ).wait_recv()
+    for copy in swaps:
+        copy.wait_send()
+
+
+def remote(kernel, number, out_shape, sems, *args, vmem=False, scratch=()):
+    space = pltpu.VMEM if vmem else pl.ANY
+    dma = pltpu.SemaphoreType.DMA
+    return pl.pallas_call(
+        kernel,
+        out_shape=out_shape,
+        in_specs=[pl.BlockSpec(memory_space=space)] * len(args),
+        out_specs=jax.tree.map(lambda _: pl.BlockSpec(memory_space=space), out_shape),
+        scratch_shapes=[*scratch, *(dma(n) if n else dma for n in sems)],
+        compiler_params=pltpu.CompilerParams(
+            collective_id=number, has_side_effects=True, vmem_limit_bytes=32 << 20
+        ),
+    )(*args)
+
+
+def bf(*shape):
+    return jax.ShapeDtypeStruct(shape, jnp.bfloat16)
+
+
 def local(n_a, n_b, tokens, norm_gain, doc_ids, q_weight, k_weight, v_weight, o_weight):
     t = tokens.shape[0]
     q_cols, kv_cols = q_weight.shape[1] // n_a, k_weight.shape[1] // n_a
@@ -121,12 +423,20 @@
         [w.reshape(t if w.shape[0] == t else w.shape[0], n_a, -1) for w in (q_weight, k_weight, v_weight)], axis=2
     ).transpose(1, 0, 2)
     w_rows = w_local.shape[1]
-    part = lax.all_to_all(w_local, "a", 0, 0) if n_a > 1 else w_local
-    weight = lax.all_gather(part, "b", axis=1).reshape(n_a * n_b * w_rows, cols)
-
-    half = lax.all_gather(tokens, "a", axis=0, tiled=True)
-    whole = lax.all_gather(half, "tp", axis=1, tiled=True)
-    gain_whole = lax.all_gather(norm_gain, "tp", axis=0, tiled=True)
+    direct = n_a > 1
+    if direct:
+        weight, whole, gain_whole = remote(
+            functools.partial(input_kernel, n_a, n_b), 1,
+            (bf(n_a, n_b, w_rows, cols), bf(n_a * t, 2 * tokens.shape[1]), bf(16, 2 * tokens.shape[1])),
+            [(3,), (n_a,), (n_a,), (n_a, n_b), (n_a, n_b), (n_a,), (n_a,), (n_a,), (n_a,), (n_a,), None, None],
+            w_local, tokens, jnp.broadcast_to(norm_gain[None], (16, norm_gain.shape[0])),
+        )
+        gain_whole = gain_whole[0]
+    else:
+        weight = lax.all_gather(w_local, "b", axis=1)
+        whole = lax.all_gather(tokens, "tp", axis=1, tiled=True)
+        gain_whole = lax.all_gather(norm_gain, "tp", axis=0, tiled=True)
+    weight = weight.reshape(n_a * n_b * w_rows, cols)
     docs = lax.all_gather(doc_ids, ("a", "b"), axis=0, tiled=True)
 
     x_float = whole.astype(jnp.float32)
@@ -140,7 +450,14 @@
     rot = rot.astype(jnp.bfloat16).reshape(rows, q_cols + kv_cols)
     q_rot = rot[:, :q_cols]
     kv = jnp.concatenate([rot[:, q_cols:], qkv[:, q_cols + kv_cols :].astype(jnp.bfloat16)], axis=1)
-    kv = lax.all_gather(kv.reshape(n_a, t, 2 * kv_cols), "b", axis=1).reshape(n_a * n_b * t, 2 * kv_cols)
+    kv = kv.reshape(n_a, t, 2 * kv_cols)
+    if direct:
+        kv = remote(
+            functools.partial(kv_kernel, n_b), 2, bf(n_a, n_b, t, 2 * kv_cols), [None, (n_b,), (n_b,)], kv
+        )
+    else:
+        kv = lax.all_gather(kv, "b", axis=1)
+    kv = kv.reshape(n_a * n_b * t, 2 * kv_cols)
 
     docq = lax.dynamic_index_in_dim(docs.reshape(n_a, n_b, t), b, 1, keepdims=False)
     chunk = t * min(4, n_a * n_b)
@@ -149,11 +466,24 @@
         q_rot, kv, docq.reshape(rows, 1), docs[None], lo, b.astype(jnp.int32)[None], n_a, n_b, kv_heads, group, chunk
     )
 
-    o_whole = lax.all_gather(o_weight, "b", axis=1, tiled=True)
-    att_whole = lax.all_gather(attended, "a", axis=1, tiled=True)
+    if direct:
+        att_whole, o_whole = remote(
+            functools.partial(wide_kernel, n_a, n_b), 3,
+            (bf(rows, n_a * q_cols), bf(o_weight.shape[0], n_b * o_weight.shape[1])),
+            [(2,), (n_a,), (n_a,), (n_a,), (n_b,), (n_b,)],
+            attended, o_weight,
+        )
+    else:
+        att_whole, o_whole = attended, lax.all_gather(o_weight, "b", axis=1, tiled=True)
     partial = jnp.dot(att_whole, o_whole, preferred_element_type=jnp.float32).astype(jnp.bfloat16)
-    if n_a > 1:
-        partial = lax.all_to_all(partial.reshape(n_a, t, -1), "a", 0, 0).transpose(1, 0, 2).reshape(t, -1)
+    if direct:
+        half, w = n_a // 2, partial.shape[1]
+        return remote(
+            functools.partial(final_kernel, n_a), 4, bf(t, half * w),
+            [(half,), (half,), (half,), (half,), None],
+            partial.reshape(n_a, t, w), vmem=True,
+            scratch=(pltpu.VMEM((half, t, w), jnp.bfloat16), pltpu.VMEM((half, t, w), jnp.bfloat16)),
+        )
     return lax.psum_scatter(partial, "tp", scatter_dimension=1, tiled=True)
 
 
@@ -161,7 +491,7 @@
     n_ctx, n_tp = mesh.shape["ctx"], mesh.shape["tp"]
 
     def run(tokens, norm_gain, doc_ids, q_weight, k_weight, v_weight, o_weight):
-        n_a = math.gcd(math.gcd(k_weight.shape[1] // n_tp // HEAD, n_ctx), 4)
+        n_a = math.gcd(math.gcd(k_weight.shape[1] // n_tp // HEAD, n_ctx), 4) if n_tp == 2 else 1
         n_b = n_ctx // n_a
         grid = Mesh(mesh.devices.reshape(n_a, n_b, n_tp), ("a", "b", "tp"))
         ctx = ("a", "b")

time: 482 us -> 327 us (0.68)
  Pallas kernels: 27.2 us -> 250 us
  waiting for transfers between devices: 219 us -> 0 us
  blocking collectives: 178 us -> 39.1 us
  between operations: 13.7 us -> 0.33 us
    pallas_call x0 -> x4, Pallas kernels: none -> 224 us  [remote(): pl.pallas_call(kernel, out_shape=out_shape, in_specs=[pl.BlockSpec(memory...]
    all_gather x6 -> x0, waiting for transfers between devices: 208 us -> none  [the longest x1 82.2 us: local(): att_whole = lax.all_gather(attended, 'a', axis=1, tiled=True)]
    all_to_all x2 -> x0, blocking collectives: 135 us -> none  [the longest x1 84.4 us: local(): part = lax.all_to_all(w_local, 'a', 0, 0) if n_a > 1 else w_local]
    reduce_scatter x1 -> x0, waiting for transfers between devices: 8.79 us -> none  [local(): return lax.psum_scatter(partial, 'tp', scatter_dimension=1, tiled=True)]
    all_gather x1 -> x0, local copies, waits for them, and re-layouts: 8.77 us -> none  [local(): weight = lax.all_gather(part, 'b', axis=1).reshape(n_a * n_b * w_rows, cols)]
  transfers between devices with their start and end apart: 7 -> 0, of which waited for: 6 -> 0; matrix products, arithmetic and copies ran while one was open for 3% -> 0% of each run, Pallas kernels for 6% -> 0%
where the time goes in v2:
time: 327 us; the launch traced here: 323 us
  Pallas kernels  250 us (76%)
  blocking collectives  39.1 us (12%)
  local copies, waits for them, and re-layouts  16.1 us (5%)
  matrix products  13.7 us (4%)
  other arithmetic  3.79 us (1%)
    pallas_call x4, Pallas kernels, remote(): pl.pallas_call(kernel, out_shape=out_shape, in_specs=[pl.BlockSpec(memory...  224 us
    all_gather x1, blocking collectives, local(): docs = lax.all_gather(doc_ids, ('a', 'b'), axis=0, tiled=True)  39.1 us
    pallas_call x1, Pallas kernels, flash(): pl.pallas_call(functools.partial(flash_kernel, kv_heads, group, chunk, n_...  26.5 us
    unnamed x29, local copies, waits for them, and re-layouts  9.46 us
    dot_general x1, matrix products, local(): qkv = jnp.dot(normed, weight, preferred_element_type=jnp.float32)  9 us

profile of v2, /device:TPU:0, one launch (start us, length us, event | category | flops | bytes accessed | tf_op | source)
XLA Modules:
  0.0 323.2 jit_solution(4893753498454791963)
XLA Ops:
  0.0 0.0 copy-start.7
  0.0 0.0 copy-start.8
  0.0 1.5 copy.49
  1.5 0.5 copy.52
  2.1 0.0 copy-done.7
  2.1 0.0 copy-start.9
  2.1 0.0 copy-start.2
  2.1 0.1 copy.50
  2.3 0.2 copy.53
  2.4 0.0 copy-done.8
  2.5 0.1 copy.51
  2.6 0.2 copy.54
  2.8 0.1 maximum_bitcast_fusion.w_ref
  2.9 0.0 copy-done.9
  2.9 0.4 copy-done.2
  3.3 111.4 %shard_map.73 = (bf16[4,4,256,768]{3,2,1,0:T(8,128)(2,1)S(1)}, bf16[1024,4096]{1,0:T(8,128)(2,1)S(1)}, bf16[16,4096]{1,0:T(8,128)(2,1)S(1)}) custom-call(bf16[4,256,768]{2,1,0:T(8,128)(2,1)S(1)} %maximum_bitcast_fusion.w_ref, bf16[256,2048]{1,0:T(8,128)(2,1)S(1)} %copy-done.2, bf16[16,2048]{1,0:T(8,128)(2,1)S(1)} %broadcast_in_dim.7.gain_ref), custom_call_target="tpu_custom_call" | custom-call | tf_op jit(solution)/shard_map/pallas_call | solution.py:398
  114.8 0.0 copy-start.3
  114.8 2.6 copy-done.3
  117.4 0.0 copy-start.4
  117.4 1.7 fusion
  119.1 1.1 copy-done.4
  120.2 9.0 %fusion.3 = f32[1024,768]{0,1:T(8,128)} fusion(bf16[4096,768]{1,0:T(8,128)(2,1)S(1)} %bitcast.31, bf16[1024,4096]{1,0:T(8,128)(2,1)S(1)} %get-tuple-element.10, f32[4096]{0:T(1024)S(1)} %bitcast.40, f32[1024]{0:T(1024)S(1)} %add_rsqrt_fusion), kind=kOutput, calls=%fused_computation.5 | convolution fusion | flops 6459228160 | bytes 17846272 | tf_op jit(solution)/shard_map/dot_general | solution.py:445
  129.2 1.9 slice.34
  131.1 0.1 convert_bitcast_fusion
  131.2 1.0 multiply_cosine_fusion
  132.2 0.4 subtract_convert_fusion
  132.7 0.1 pad_maximum_fusion
  132.8 0.0 copy-start.5
  132.8 1.5 slice.47
  134.3 0.0 copy-done.5
  134.4 0.2 copy.56
  134.6 0.0 copy-start.6
  134.6 0.0 copy-start.10
  134.6 26.3 %shard_map.74 = bf16[4,4,256,256]{3,2,1,0:T(8,128)(2,1)S(1)} custom-call(bf16[4,256,256]{2,1,0:T(8,128)(2,1)S(1)} %bitcast.27), custom_call_target="tpu_custom_call" | custom-call | tf_op jit(solution)/shard_map/pallas_call | solution.py:398
  160.9 0.0 copy-done.6
  160.9 1.0 slice.37
  162.0 1.5 copy.60.q_ref
  163.5 0.0 copy-done.10
  163.5 39.1 %all-gather = s32[16,1,256]{2,1,0:T(1,128)S(1)} all-gather(s32[1,1,256]{2,1,0:T(1,128)S(1)} %bitcast.42), channel_id=1, replica_groups=mesh['a'=4,'b'=4,'tp'=2] {'a','b'}, dimensions={0}, use_global_device_ids=true | all-gather | bytes 17408 | tf_op jit(solution)/shard_map/all_gather | solution.py:440
  202.7 0.1 slice_reduce_fusion
  202.8 0.2 convert_reduce_fusion
  203.0 1.0 copy.57.docq_ref
  204.0 0.0 copy-start
  204.0 1.0 copy-done
  205.1 0.0 copy-start.1
  205.1 26.5 %shard_map.75.att_ref = bf16[1024,512]{1,0:T(8,128)(2,1)S(1)} custom-call(s32[4]{0:T(128)S(1)} %and_select_fusion.lo_ref, s32[1]{0:T(128)} %bitcast.2.b_ref, bf16[1024,512]{1,0:T(8,128)(2,1)S(1)} %copy.60.q_ref, bf16[4096,256]{1,0:T(8,128)(2,1)S(1)} %bitcast.26, s32[1024,1]{1,0:T(8,128)S(1)} %copy-done, s32[1,4096]{1,0:T(1,128)S(1)} %bitcast.30), custom_call_target="tpu_custom_call" | custom-call | tf_op jit(solution)/shard_map/pallas_call | solution.py:90
  231.6 0.0 copy-done.1
  231.6 62.8 %shard_map.76 = (bf16[1024,2048]{1,0:T(8,128)(2,1)S(1)}, bf16[2048,1024]{1,0:T(8,128)(2,1)S(1)}) custom-call(bf16[1024,512]{1,0:T(8,128)(2,1)S(1)} %shard_map.75.att_ref, bf16[2048,256]{1,0:T(8,128)(2,1)S(1)} %copy-done.1), custom_call_target="tpu_custom_call" | custom-call | tf_op jit(solution)/shard_map/pallas_call | solution.py:398
  294.4 4.7 %convolution_convert_fusion = bf16[1024,1024]{1,0:T(8,128)(2,1)S(1)} fusion(bf16[1024,2048]{1,0:T(8,128)(2,1)S(1)} %get-tuple-element.13, bf16[2048,1024]{1,0:T(8,128)(2,1)S(1)} %get-tuple-element.14), kind=kOutput, calls=%fused_computation.8 | convolution fusion | flops 4296015872 | bytes 10485760 | tf_op jit(solution)/shard_map/dot_general | solution.py:478
  299.1 23.1 %shard_map.77 = bf16[256,2048]{1,0:T(8,128)(2,1)S(1)} custom-call(bf16[4,256,1024]{2,1,0:T(8,128)(2,1)S(1)} %bitcast.28), custom_call_target="tpu_custom_call" | custom-call | tf_op jit(solution)/shard_map/pallas_call | solution.py:398
  322.2 1.0 copy.65
  (13 shorter events, 0.2 us)
Async XLA Ops:
  0.0 2.1 copy-start.7
  0.0 2.4 copy-start.8
  2.1 0.8 copy-start.9
  2.1 1.2 copy-start.2
  114.8 2.6 copy-start.3
  117.4 2.8 copy-start.4
  132.8 1.5 copy-start.5
  134.6 26.4 %copy-start.6 = (bf16[1024,5,128]{0,2,1:T(8,128)(2,1)S(1)}, bf16[1024,5,128]{0,2,1:T(8,128)(2,1)}, u32[]{:S(2)}) copy-start(bf16[1024,5,128]{0,2,1:T(8,128)(2,1)} %copy-done.5) | copy-start | bytes 3932164
  134.6 28.9 %copy-start.10 = (s32[256]{0:T(256)S(1)}, s32[256]{0:T(256)}, u32[]{:S(2)}) copy-start(s32[256]{0:T(256)} %param.9) | copy-start | bytes 3076
  204.0 1.0 copy-start
  205.1 26.5 %copy-start.1 = (bf16[2048,256]{1,0:T(8,128)(2,1)S(1)}, bf16[2048,256]{1,0:T(8,128)(2,1)}, u32[]{:S(2)}) copy-start(bf16[2048,256]{1,0:T(8,128)(2,1)} %o_ref.1) | copy-start | bytes 3145732

commit v3 on v2

--- a/solution.py
+++ b/solution.py
@@ -188,8 +188,8 @@
 
 
 def input_kernel(
-    n_a, n_b, w_ref, tok_ref, gain_ref, weight_ref, whole_ref, gain_out,
-    own_sem, z_send, z_recv, p_send, p_recv, right_sem, left_sem, t_recv, c_send, c_recv, g_send, g_recv,
+    n_a, n_b, w_ref, tok_ref, gain_ref, doc_ref, weight_ref, whole_ref, gain_out, doc_out,
+    own_sem, z_send, z_recv, p_send, p_recv, right_sem, left_sem, t_recv, c_send, c_recv, g_send, g_recv, d_send, d_recv,
 ):
     a, b, c = lax.axis_index("a"), lax.axis_index("b"), lax.axis_index("tp")
     t, width = tok_ref.shape
@@ -208,6 +208,8 @@
     for o in range(1, n_a):
         to = place(n_a, "a", o)
         exchange.append(push(w_ref.at[to], weight_ref.at[a, b], z_send.at[o - 1], z_recv.at[a], "a", to))
+        exchange[-1].start()
+        exchange.append(push(doc_ref, doc_out.at[a], d_send.at[o - 1], d_recv.at[a], "a", to))
         exchange[-1].start()
 
     def cross(k, side, index):
@@ -235,6 +237,7 @@
         pltpu.make_async_copy(w_ref.at[a], weight_ref.at[a, b], own_sem.at[0]),
         pltpu.make_async_copy(tok_ref, spot(a), own_sem.at[1]),
         pltpu.make_async_copy(gain_ref, gain_spot(c), own_sem.at[2]),
+        pltpu.make_async_copy(doc_ref, doc_out.at[a], own_sem.at[3]),
     ]
     for copy in own:
         copy.start()
@@ -255,6 +258,9 @@
     for index in range(n_a):
         push(spot(index), spot(index, other), c_send.at[index], c_recv.at[index], "tp", other).wait_recv()
     push(gain_ref, gain_spot(other), g_send, g_recv, "tp", other).wait_recv()
+    for k in range(1, n_a):
+        index = place(n_a, "a", k)
+        push(doc_ref, doc_out.at[index], d_send.at[k - 1], d_recv.at[index], "a", index).wait_recv()
     for copy in exchange:
         copy.wait_send()
     for k in range(n_a):
@@ -268,22 +274,28 @@
         copy.wait()
 
 
-def kv_kernel(n_b, kv_ref, out_ref, own_sem, send, recv):
+def kv_kernel(n_b, kv_ref, doc_ref, out_ref, doc_out, own_sem, send, recv, d_send, d_recv):
     b = lax.axis_index("b")
     greet({"b": n_b})
-    copies = [
-        push(kv_ref, out_ref.at[:, b], send.at[o - 1], recv.at[b], "b", place(n_b, "b", o)) for o in range(1, n_b)
+    copies = []
+    for o in range(1, n_b):
+        to = place(n_b, "b", o)
+        copies.append(push(kv_ref, out_ref.at[:, b], send.at[o - 1], recv.at[b], "b", to))
+        copies.append(push(doc_ref, doc_out.at[:, b], d_send.at[o - 1], d_recv.at[b], "b", to))
+    own = [
+        pltpu.make_async_copy(kv_ref, out_ref.at[:, b], own_sem.at[0]),
+        pltpu.make_async_copy(doc_ref, doc_out.at[:, b], own_sem.at[1]),
     ]
-    for copy in copies:
+    for copy in copies + own:
         copy.start()
-    own = pltpu.make_async_copy(kv_ref, out_ref.at[:, b], own_sem)
-    own.start()
     for o in range(1, n_b):
         source = place(n_b, "b", o)
         push(kv_ref, out_ref.at[:, source], send.at[o - 1], recv.at[source], "b", source).wait_recv()
+        push(doc_ref, doc_out.at[:, source], d_send.at[o - 1], d_recv.at[source], "b", source).wait_recv()
     for copy in copies:
         copy.wait_send()
-    own.wait()
+    for copy in own:
+        copy.wait()
 
 
 def wide_kernel(n_a, n_b, att_ref, o_ref, att_out, o_out, own_sem, right_sem, left_sem, t_recv, send, recv):
@@ -425,11 +437,13 @@
     w_rows = w_local.shape[1]
     direct = n_a > 1
     if direct:
-        weight, whole, gain_whole = remote(
+        weight, whole, gain_whole, doc_column = remote(
             functools.partial(input_kernel, n_a, n_b), 1,
-            (bf(n_a, n_b, w_rows, cols), bf(n_a * t, 2 * tokens.shape[1]), bf(16, 2 * tokens.shape[1])),
-            [(3,), (n_a,), (n_a,), (n_a, n_b), (n_a, n_b), (n_a,), (n_a,), (n_a,), (n_a,), (n_a,), None, None],
+            (bf(n_a, n_b, w_rows, cols), bf(n_a * t, 2 * tokens.shape[1]), bf(16, 2 * tokens.shape[1]),
+             jax.ShapeDtypeStruct((n_a, 8, t), jnp.int32)),
+            [(4,), (n_a,), (n_a,), (n_a, n_b), (n_a, n_b), (n_a,), (n_a,), (n_a,), (n_a,), (n_a,), None, None, (n_a,), (n_a,)],
             w_local, tokens, jnp.broadcast_to(norm_gain[None], (16, norm_gain.shape[0])),
+            jnp.broadcast_to(doc_ids[None], (8, t)),
         )
         gain_whole = gain_whole[0]
     else:
@@ -437,7 +451,6 @@
         whole = lax.all_gather(tokens, "tp", axis=1, tiled=True)
         gain_whole = lax.all_gather(norm_gain, "tp", axis=0, tiled=True)
     weight = weight.reshape(n_a * n_b * w_rows, cols)
-    docs = lax.all_gather(doc_ids, ("a", "b"), axis=0, tiled=True)
 
     x_float = whole.astype(jnp.float32)
     mean_sq = jnp.mean(x_float * x_float, axis=-1, keepdims=True)
@@ -452,14 +465,17 @@
     kv = jnp.concatenate([rot[:, q_cols:], qkv[:, q_cols + kv_cols :].astype(jnp.bfloat16)], axis=1)
     kv = kv.reshape(n_a, t, 2 * kv_cols)
     if direct:
-        kv = remote(
-            functools.partial(kv_kernel, n_b), 2, bf(n_a, n_b, t, 2 * kv_cols), [None, (n_b,), (n_b,)], kv
+        kv, docs = remote(
+            functools.partial(kv_kernel, n_b), 2,
+            (bf(n_a, n_b, t, 2 * kv_cols), jax.ShapeDtypeStruct((n_a, n_b, 8, t), jnp.int32)),
+            [(2,), (n_b,), (n_b,), (n_b,), (n_b,)], kv, doc_column,
         )
+        docs, docq = docs[:, :, 0].reshape(-1), doc_column[:, 0]
     else:
+        docs, docq = lax.all_gather(doc_ids, "b", axis=0, tiled=True), doc_ids[None]
         kv = lax.all_gather(kv, "b", axis=1)
     kv = kv.reshape(n_a * n_b * t, 2 * kv_cols)
 
-    docq = lax.dynamic_index_in_dim(docs.reshape(n_a, n_b, t), b, 1, keepdims=False)
     chunk = t * min(4, n_a * n_b)
     lo = jnp.sum((docs[None, :] < docq[:, :1]).astype(jnp.int32), axis=1) // chunk
     attended = flash(

time: 327 us -> 300 us (0.917)
  blocking collectives: 39.1 us -> 0 us
  Pallas kernels: 250 us -> 261 us
    all_gather x1 -> x0, blocking collectives: 39.1 us -> none  [local(): docs = lax.all_gather(doc_ids, ('a', 'b'), axis=0, tiled=True)]
    pallas_call x4, Pallas kernels: 224 us -> 234 us  [remote(): pl.pallas_call(kernel, out_shape=out_shape, in_specs=[pl.BlockSpec(memory...]
    unnamed x29 -> x27, local copies, waits for them, and re-layouts: 9.46 us -> 10 us
where the time goes in v3:
time: 300 us; the launch traced here: 296 us
  Pallas kernels  261 us (87%)
  local copies, waits for them, and re-layouts  16.3 us (5%)
  matrix products  14.4 us (5%)
  other arithmetic  3.75 us (1%)
    pallas_call x4, Pallas kernels, remote(): pl.pallas_call(kernel, out_shape=out_shape, in_specs=[pl.BlockSpec(memory...  234 us
    pallas_call x1, Pallas kernels, flash(): pl.pallas_call(functools.partial(flash_kernel, kv_heads, group, chunk, n_...  26.5 us
    unnamed x27, local copies, waits for them, and re-layouts  10 us
    dot_general x1, matrix products, local(): qkv = jnp.dot(normed, weight, preferred_element_type=jnp.float32)  9.71 us

profile of v3, /device:TPU:0, one launch (start us, length us, event | category | flops | bytes accessed | tf_op | source)
XLA Modules:
  0.0 295.8 jit_solution(17462269216301497029)
XLA Ops:
  0.0 0.0 copy-start.6
  0.0 0.0 copy-start.7
  0.0 1.5 copy.20
  1.5 0.5 copy.23
  2.1 0.0 copy-done.6
  2.1 0.0 copy-start.8
  2.1 0.0 copy-start.9
  2.1 0.0 copy-start.2
  2.1 0.1 copy.21
  2.3 0.2 copy.24
  2.5 0.0 copy-done.7
  2.5 0.1 copy.22
  2.6 0.2 copy.25
  2.8 0.1 maximum_bitcast_fusion.w_ref
  2.9 0.0 copy-done.8
  2.9 0.0 copy-done.9
  3.0 0.4 copy-done.2
  3.4 112.2 %shard_map.73 = (bf16[4,4,256,768]{3,2,1,0:T(8,128)(2,1)S(1)}, bf16[1024,4096]{1,0:T(8,128)(2,1)S(1)}, bf16[16,4096]{1,0:T(8,128)(2,1)S(1)}, s32[4,8,256]{2,1,0:T(8,128)S(1)}) custom-call(bf16[4,256,768]{2,1,0:T(8,128)(2,1)S(1)} %maximum_bitcast_fusion.w_ref, bf16[256,2048]{1,0:T(8,128)(2,1)S(1)} %copy-done.2, ...), custom_call_target="tpu_custom_call" | custom-call | tf_op jit(solution)/shard_map/pallas_call | solution.py:410
  115.6 0.0 copy-start.3
  115.6 2.7 copy-done.3
  118.2 1.7 fusion
  120.0 9.7 %fusion.3 = f32[1024,768]{0,1:T(8,128)S(1)} fusion(bf16[4096,768]{1,0:T(8,128)(2,1)} %bitcast.30, bf16[1024,4096]{1,0:T(8,128)(2,1)S(1)} %get-tuple-element.13, f32[4096]{0:T(1024)S(1)} %bitcast.39, f32[1024]{0:T(1024)S(1)} %add_rsqrt_fusion), kind=kOutput, calls=%fused_computation.5 | convolution fusion | flops 6459228160 | bytes 17846272 | tf_op jit(solution)/shard_map/dot_general | solution.py:458
  129.7 0.0 copy-start.5
  129.7 1.6 copy-done.5
  131.3 0.3 slice.41
  131.6 0.1 convert_bitcast_fusion
  131.7 1.0 multiply_cosine_fusion
  132.7 0.4 subtract_convert_fusion
  133.2 0.1 pad_maximum_fusion
  133.3 0.0 copy-start.4
  133.4 1.5 slice.55
  134.8 0.0 copy-done.4
  134.9 0.2 copy.26
  135.1 27.8 %shard_map.74 = (bf16[4,4,256,256]{3,2,1,0:T(8,128)(2,1)S(1)}, s32[4,4,8,256]{3,2,1,0:T(8,128)S(1)}) custom-call(bf16[4,256,256]{2,1,0:T(8,128)(2,1)S(1)} %bitcast.26, s32[4,8,256]{2,1,0:T(8,128)S(1)} %get-tuple-element.16.doc_ref), custom_call_target="tpu_custom_call" | custom-call | tf_op jit(solution)/shard_map/pallas_call | solution.py:410
  163.0 0.1 slice_reduce_fusion
  163.1 0.2 convert_reduce_fusion
  163.3 2.3 slice.47
  165.6 1.5 copy.30.q_ref
  167.1 1.0 copy.28.docq_ref
  168.1 0.0 copy-start
  168.1 1.0 copy-done
  169.2 0.0 copy-start.1
  169.2 26.5 %shard_map.75.att_ref = bf16[1024,512]{1,0:T(8,128)(2,1)S(1)} custom-call(s32[4]{0:T(128)S(1)} %and_select_fusion.lo_ref, s32[1]{0:T(128)} %bitcast.10.b_ref, bf16[1024,512]{1,0:T(8,128)(2,1)S(1)} %copy.30.q_ref, bf16[4096,256]{1,0:T(8,128)(2,1)S(1)} %bitcast.27, s32[1024,1]{1,0:T(8,128)S(1)} %copy-done, s32[1,4096]{1,0:T(1,128)S(1)} %bitcast.29), custom_call_target="tpu_custom_call" | custom-call | tf_op jit(solution)/shard_map/pallas_call | solution.py:90
  195.7 0.0 copy-done.1
  195.7 71.8 %shard_map.76 = (bf16[1024,2048]{1,0:T(8,128)(2,1)S(1)}, bf16[2048,1024]{1,0:T(8,128)(2,1)S(1)}) custom-call(bf16[1024,512]{1,0:T(8,128)(2,1)S(1)} %shard_map.75.att_ref, bf16[2048,256]{1,0:T(8,128)(2,1)S(1)} %copy-done.1), custom_call_target="tpu_custom_call" | custom-call | tf_op jit(solution)/shard_map/pallas_call | solution.py:410
  267.5 4.7 %convolution_convert_fusion = bf16[1024,1024]{1,0:T(8,128)(2,1)S(1)} fusion(bf16[1024,2048]{1,0:T(8,128)(2,1)S(1)} %get-tuple-element.19, bf16[2048,1024]{1,0:T(8,128)(2,1)S(1)} %get-tuple-element.20), kind=kOutput, calls=%fused_computation.8 | convolution fusion | flops 4296015872 | bytes 10485760 | tf_op jit(solution)/shard_map/dot_general | solution.py:494
  272.2 22.6 %shard_map.77 = bf16[256,2048]{1,0:T(8,128)(2,1)S(1)} custom-call(bf16[4,256,1024]{2,1,0:T(8,128)(2,1)S(1)} %bitcast.25), custom_call_target="tpu_custom_call" | custom-call | tf_op jit(solution)/shard_map/pallas_call | solution.py:410
  294.8 1.0 copy.35
  (13 shorter events, 0.1 us)
Async XLA Ops:
  0.0 2.1 copy-start.6
  0.0 2.5 copy-start.7
  2.1 0.8 copy-start.8
  2.1 0.8 copy-start.9
  2.1 1.2 copy-start.2
  115.6 2.7 copy-start.3
  129.7 1.7 copy-start.5
  133.3 1.5 copy-start.4
  168.1 1.0 copy-start
  169.2 26.5 %copy-start.1 = (bf16[2048,256]{1,0:T(8,128)(2,1)S(1)}, bf16[2048,256]{1,0:T(8,128)(2,1)}, u32[]{:S(2)}) copy-start(bf16[2048,256]{1,0:T(8,128)(2,1)} %o_ref.1) | copy-start | bytes 3145732
